TPU v7x, 128 devices: a whole 4x4x4 slice. The times are simulated.
128 devices in a mesh: occ: 8 (over z_lo, x), vir: 16 (over z_hi, y, core).
Axes of the slice: x: 4, y: 4, z: 4 (z_hi: 2, z_lo: 2; z = z_hi * 2 + z_lo), core: 2. Of those that a mesh axis runs over, the one named last changes fastest.
Arguments:
- integrals: float32 [2048, 130816], P('occ', 'vir'), may hold values from -0.0234375 to 0.0234375
- amplitudes: float32 [2016, 130816], P('occ', 'vir'), may hold values from -6 to 6
- residual_in: float32 [2016, 2048], P('occ', 'vir'), may hold values from -6 to 6
Outputs:
- residual_out: float32 [2016, 2048], P('occ', 'vir')
All inputs are finite; a program needn't handle non-finite values.
Results may differ from a plain program's by a relative error of at most 0.000075.
Values sent between devices are 32-bit elements; how exact they have to be, the bound alone decides.
A program may use at most 128 MiB of HBM per device.

v0:
```python
import jax
import jax.numpy as jnp
from jax import lax
from jax.sharding import PartitionSpec as P


def contract(left, right):
    return lax.dot_general(
        left,
        right,
        (((1,), (1,)), ((), ())),
        precision=lax.Precision.HIGHEST,
        preferred_element_type=jnp.float32,
    )


def body(integrals, amplitudes, residual_in):
    amplitude_rows, integral_rows = (
        lax.all_to_all(amplitudes, "occ", split_axis=1, concat_axis=0, tiled=True),
        lax.all_to_all(integrals, "occ", split_axis=1, concat_axis=0, tiled=True),
    )
    partial_value = lax.psum_scatter(
        contract(integral_rows, amplitude_rows), "vir", scatter_dimension=0, tiled=True
    )
    summed = lax.psum_scatter(partial_value.T, "occ", scatter_dimension=0, tiled=True)
    return residual_in + summed


def solution(mesh):
    return jax.shard_map(
        body,
        mesh=mesh,
        in_specs=(P("occ", "vir"), P("occ", "vir"), P("occ", "vir")),
        out_specs=P("occ", "vir"),
        check_vma=False,
    )
```

profile of v0, /device:TPU:32, one launch (start us, length us, event | category | flops | bytes accessed | tf_op | source)
XLA Modules:
  0.0 533.4 jit_solution(13936140675627119435)
XLA Ops:
  6.5 5.9 %reshape.6 = f32[252,8,1022]{0,2,1:T(8,128)} reshape(f32[252,8176]{0,1:T(8,128)} %param.4) | data formatting | bytes 16482816 | tf_op jit(solution)/shard_map/all_to_all | solution.py:19
  12.4 9.1 %copy.9 = f32[252,8,1022]{2,0,1:T(8,128)} copy(f32[252,8,1022]{0,2,1:T(8,128)} %reshape.6) | data formatting | bytes 16482816 | tf_op jit(solution)/shard_map/all_to_all | solution.py:19
  21.6 5.8 %all-to-all-start.1 = ((f32[252,8,1022]{2,0,1:T(8,128)}), f32[252,8,1022]{2,0,1:T(8,128)}, u32[]{:S(2)}, u32[]{:S(2)}) async-start(f32[252,8,1022]{2,0,1:T(8,128)} %copy.9), calls=%async_computation.1 | async-start | bytes 16777216 | tf_op jit(solution)/shard_map/all_to_all | solution.py:19
  27.3 5.9 %all_to_all.28 = f32[256,8,1022]{0,2,1:T(8,128)} reshape(f32[256,8176]{0,1:T(8,128)} %param.3) | data formatting | bytes 16744448 | tf_op jit(solution)/shard_map/all_to_all | solution.py:20
  33.2 87.1 %all-to-all-done.1 = f32[252,8,1022]{2,0,1:T(8,128)} async-done(((f32[252,8,1022]{2,0,1:T(8,128)}), f32[252,8,1022]{2,0,1:T(8,128)}, u32[]{:S(2)}, u32[]{:S(2)}) %all-to-all-start.1) | async-done | bytes 8241440 | tf_op jit(solution)/shard_map/all_to_all | solution.py:19
  120.3 36.5 %all-to-all-start = ((f32[256,8,1022]{0,2,1:T(8,128)}), f32[256,8,1022]{0,2,1:T(8,128)}, u32[]{:S(2)}, u32[]{:S(2)}) async-start(f32[256,8,1022]{0,2,1:T(8,128)} %all_to_all.28), calls=%async_computation | async-start | bytes 16777216 | tf_op jit(solution)/shard_map/all_to_all | solution.py:20
  156.8 0.0 reduce-scatter.4.cloned.1.call-start
  156.8 7.2 %all_to_all.35 = f32[2016,1022]{1,0:T(8,128)} reshape(f32[8,252,1022]{2,1,0:T(8,128)} %bitcast.2) | data formatting | bytes 16482816 | tf_op jit(solution)/shard_map/all_to_all | solution.py:19
  164.0 84.6 %all-to-all-done = f32[256,8,1022]{0,2,1:T(8,128)} async-done(((f32[256,8,1022]{0,2,1:T(8,128)}), f32[256,8,1022]{0,2,1:T(8,128)}, u32[]{:S(2)}, u32[]{:S(2)}) %all-to-all-start) | async-done | bytes 8372256 | tf_op jit(solution)/shard_map/all_to_all | solution.py:20
  248.6 9.1 %copy.7 = f32[8,256,1022]{2,1,0:T(8,128)} copy(f32[8,256,1022]{1,2,0:T(8,128)} %bitcast) | data formatting | bytes 16744448 | tf_op jit(solution)/shard_map/all_to_all | solution.py:20
  257.7 57.8 %fusion.1 = f32[2048,2016]{0,1:T(8,128)} fusion(f32[2048,1022]{1,0:T(8,128)} %bitcast.13, f32[2016,1022]{1,0:T(8,128)} %all_to_all.35), kind=kOutput, calls=%fused_computation.1 | convolution fusion | flops 50635210752 | bytes 33128704 | tf_op jit(solution)/shard_map/dot_general | solution.py:8
  315.5 0.0 copy-start.1
  315.5 0.0 copy-start
  315.5 0.0 reduce-scatter.4.cloned.1.call-update
  315.5 177.1 %reduce-scatter.4.cloned.1.call-done = f32[128,2016]{0,1:T(8,128)} async-done(((f32[2048,2016]{0,1:T(8,128)}), f32[128,2016]{0,1:T(8,128)}) %reduce-scatter.4.cloned.1.call-update) | async-done | bytes 1032208 | tf_op jit(solution)/shard_map/reduce_scatter | solution.py:22
  492.7 25.1 %fusion = f32[256,128]{1,0:T(8,128)S(1)} fusion(f32[2016,128]{1,0:T(8,128)} %bitcast.14), kind=kCustom, calls=%all-reduce-scatter | all-reduce-scatter fusion | flops 262145 | bytes 1163776
  517.7 3.6 collective-permute-start
  521.3 0.0 copy-done.1
  521.3 0.6 dynamic-slice.4
  522.6 2.9 collective-permute-done
  525.5 0.4 concatenate
  525.8 0.0 copy-done
  525.9 0.7 dynamic-slice_add_fusion
  (1 shorter events, 0.0 us)
Async XLA Ops:
  21.6 98.8 %all-to-all-start.1 = ((f32[252,8,1022]{2,0,1:T(8,128)}), f32[252,8,1022]{2,0,1:T(8,128)}, u32[]{:S(2)}, u32[]{:S(2)}) async-start(f32[252,8,1022]{2,0,1:T(8,128)} %copy.9), calls=%async_computation.1 | async-start | bytes 16777216 | tf_op jit(solution)/shard_map/all_to_all | solution.py:19
  120.3 128.2 %all-to-all-start = ((f32[256,8,1022]{0,2,1:T(8,128)}), f32[256,8,1022]{0,2,1:T(8,128)}, u32[]{:S(2)}, u32[]{:S(2)}) async-start(f32[256,8,1022]{0,2,1:T(8,128)} %all_to_all.28), calls=%async_computation | async-start | bytes 16777216 | tf_op jit(solution)/shard_map/all_to_all | solution.py:20
  156.8 335.9 %reduce-scatter.4.cloned.1.call-start = ((), (), s32[]{:S(2)}) async-start(), calls=%async_computation.3 | async-start | bytes 17547264 | tf_op jit(solution)/shard_map/reduce_scatter | solution.py:22
  315.5 205.8 %copy-start.1 = (u32[128]{0:T(128)S(1)}, u32[128]{0:T(128)}, u32[]{:S(2)}) copy-start(u32[128]{0:T(128)} %constant.4) | copy-start | bytes 1540
  315.5 210.3 %copy-start = (f32[252,128]{1,0:T(8,128)S(1)}, f32[252,128]{1,0:T(8,128)}, u32[]{:S(2)}) copy-start(f32[252,128]{1,0:T(8,128)} %param.5) | copy-start | bytes 387076
  517.7 7.7 %collective-permute-start = (f32[28,128]{1,0:T(8,128)S(1)}, f32[28,128]{1,0:T(8,128)S(1)}, u32[]{:S(2)}, u32[]{:S(2)}) collective-permute-start(f32[28,128]{1,0:T(8,128)S(1)} %slice), channel_id=1, source_target_pairs={{0,16},{16,32},{32,48},{48,64},{64,80},{80,96},{96,112},{1,17},{17... | collective-permute-start | bytes 43016
Sparse Core Ops, SparseCore 0:
  315.7 176.9 reduce-scatter.3
where the time goes:
time: 534 us; the launch traced here: 533 us
  waiting for transfers between devices  352 us (66%)
  matrix products  57.8 us (11%)
  starting transfers between devices  45.8 us (9%)
  local copies, waits for them, and re-layouts  38.2 us (7%)
  blocking collectives  25.1 us (5%)
  between operations  14.1 us (3%)
    reduce_scatter x1, waiting for transfers between devices, body(): lax.psum_scatter(contract(integral_rows, amplitude_rows), 'vir', scatter_...  177 us
    all_to_all x1, waiting for transfers between devices, body(): lax.all_to_all(amplitudes, 'occ', split_axis=1, concat_axis=0, tiled=True)  87.1 us
    all_to_all x1, waiting for transfers between devices, body(): lax.all_to_all(integrals, 'occ', split_axis=1, concat_axis=0, tiled=True)  84.6 us
    dot_general x1, matrix products, contract(): lax.dot_general(left, right, (((1,), (1,)), ((), ())), precision=lax.Prec...  57.8 us
    all_to_all x1, starting transfers between devices, body(): lax.all_to_all(integrals, 'occ', split_axis=1, concat_axis=0, tiled=True)  36.5 us
    unnamed x1, blocking collectives  25.1 us
    all_to_all x3, local copies, waits for them, and re-layouts, body(): lax.all_to_all(amplitudes, 'occ', split_axis=1, concat_axis=0, tiled=True)  22.2 us
    all_to_all x2, local copies, waits for them, and re-layouts, body(): lax.all_to_all(integrals, 'occ', split_axis=1, concat_axis=0, tiled=True)  15 us
  transfers between devices with their start and end apart: 4, of which 4 were waited for; matrix products, arithmetic and copies ran while one was open for 0% of the time, Pallas kernels for 0%

commit v1 on v0

v1 whole, which is shorter than its diff:
```python
import jax
import jax.numpy as jnp
from jax import lax
from jax.experimental import pallas as pl
from jax.experimental.pallas import tpu as pltpu
from jax.sharding import PartitionSpec as P

MESH = pl.DeviceIdType.MESH
F32, BF16 = jnp.float32, jnp.bfloat16
NT = (((1,), (1,)), ((), ()))

ROWS, HALF, QUARTER, LANES = 256, 128, 2048, 128
SLOTS = 8

OFFSET = (0, -1, 1, 2)


def dot(a, b):
    return lax.dot_general(a, b, NT, preferred_element_type=F32)


def kernel(
    amp, amp_cols, amp_rows, itg, itg_cols, residual, out,
    vx, vz, ax, stage, vhi, vlo, ahi, alo, ptile, crecv, yrecv, xrecv, total, zsend, zrecv,
    own_sem, gsend, grecv_v, grecv_a, fsend, frecv, csend, crecv_sem, ysend, yrecv_sem,
    osend, orecv, zsem,
):
    occ, vir = lax.axis_index("occ"), lax.axis_index("vir")
    x, zl = lax.rem(occ, 4), occ // 4
    core, y, zh = lax.rem(vir, 2), lax.rem(vir // 2, 4), vir // 8

    def at(dx=0, dzl=0, dy=0, dzh=0, dc=0):
        return (
            lax.rem(zl + dzl, 2) * 4 + lax.rem(x + dx + 4, 4),
            lax.rem(zh + dzh, 2) * 8 + lax.rem(y + dy + 4, 4) * 2 + lax.rem(core + dc, 2),
        )

    peers = [at(dx=1), at(dx=-1), at(dx=2), at(dzl=1), at(dc=1), at(dy=1), at(dy=-1), at(dy=2), at(dzh=1)]
    barrier = pltpu.get_barrier_semaphore()
    for peer in peers:
        pl.semaphore_signal(barrier, inc=1, device_id=peer, device_id_type=MESH)
    pl.semaphore_wait(barrier, len(peers))

    def remote(src, dst, ssem, rsem, device):
        pltpu.make_async_remote_copy(
            src_ref=src, dst_ref=dst, send_sem=ssem, recv_sem=rsem, device_id=device, device_id_type=MESH
        ).start()

    def wait(ref, sem):
        pltpu.make_async_copy(ref, ref, sem).wait()

    def spread(array, cols, rows, half, quarter, dst, make):
        r0 = half * HALF
        n = HALF if rows is None or half == 0 else HALF - 8

        @pl.when(quarter != 3)
        def _():
            at_col = pl.multiple_of(quarter * QUARTER, LANES)
            make(array.at[pl.ds(r0, n), pl.ds(at_col, QUARTER)], dst.at[pl.ds(0, n)])

        @pl.when(quarter == 3)
        def _():
            main = QUARTER - LANES
            make(array.at[pl.ds(r0, n), pl.ds(3 * QUARTER, main)], dst.at[pl.ds(0, n), pl.ds(0, main)])
            make(cols.at[pl.ds(r0, n)], dst.at[pl.ds(0, n), pl.ds(main, LANES)])

        if n != HALF:
            at_col = pl.multiple_of(quarter * QUARTER, LANES)
            make(rows.at[:, pl.ds(at_col, QUARTER)], dst.at[pl.ds(n, 8)])

    def send(kind, half, dx, s):
        quarter = lax.rem(x + dx + 4, 4)
        device = at(dx=dx)
        if kind == "v":
            ssem, rsem = gsend.at[s, half], grecv_v.at[s, half]
            spread(itg, itg_cols, None, half, quarter, vx.at[s, half], lambda a, b: remote(a, b, ssem, rsem, device))
        else:
            ssem, rsem = gsend.at[s, 2 + half], grecv_a.at[s, half]
            dst = ax.at[s, pl.ds(half * HALF, HALF)]
            spread(amp, amp_cols, amp_rows, half, quarter, dst, lambda a, b: remote(a, b, ssem, rsem, device))

    def send_near(kind, half):
        send(kind, half, 1, 0)
        send(kind, half, -1, 1)

    def send_far(kind, half):
        send(kind, half, 2, 2)

    def forward(s, half):
        remote(vx.at[s, half], vz.at[s + 1, half], fsend.at[s + 1, half], frecv.at[s + 1, half], at(dzl=1))

    def split(src, hi, lo):
        def step(c, _):
            rows = pl.ds(pl.multiple_of(c * 32, 32), 32)
            value = src[rows]
            high = value.astype(BF16)
            hi[rows] = high
            lo[rows] = (value - high.astype(F32)).astype(BF16)
            return 0

        lax.fori_loop(0, HALF // 32, step, 0)

    def split_v(src, j, half):
        rows = pl.ds(half * HALF, HALF)
        split(src, vhi.at[j, rows], vlo.at[j, rows])

    def split_a(src, i, half):
        rows = pl.ds(half * HALF, HALF)
        split(src, ahi.at[i, rows], alo.at[i, rows])

    def take_v(s, half):
        wait(vx.at[s, half], grecv_v.at[s, half])
        forward(s, half)

    def take_z(s, half):
        wait(vz.at[s, half], frecv.at[s, half])
        split_v(vz.at[s, half], 4 + s, half)

    def take_a(s, half):
        rows = pl.ds(half * HALF, HALF)
        wait(ax.at[s, rows], grecv_a.at[s, half])
        split_a(ax.at[s, rows], s + 1, half)

    def rows_of(half):
        return pl.ds(0, ROWS) if half is None else pl.ds(half * HALF, HALF)

    def sem_row(i, half):
        return i if half is None else 3 + half

    def produce(i, j, half, slot, free):
        rows = rows_of(half)
        n = ROWS if half is None else HALF
        if not free:
            wait(ptile.at[slot, 0, pl.ds(0, n)], csend.at[slot])
        high, low = ahi[i, rows], alo[i, rows]
        both = jnp.concatenate([high, low], axis=0)
        one = dot(both, vhi[j])
        if half is None:
            value = one[:n] + one[n:] + dot(high, vlo[j])
        else:
            two = dot(both, vlo[j])
            value = one[:n] + one[n:] + two[:n] + two[n:]
        ptile[slot, 0, pl.ds(0, n)] = value[:, :LANES]
        ptile[slot, 1, pl.ds(0, n)] = value[:, LANES:]
        remote(
            ptile.at[slot, 1 - core, pl.ds(0, n)], crecv.at[j, i, rows],
            csend.at[slot], crecv_sem.at[j, sem_row(i, half)], at(dc=1),
        )

    def finish(i, j, half, slot):
        rows = rows_of(half)
        n = ROWS if half is None else HALF
        wait(crecv.at[j, i, rows], crecv_sem.at[j, sem_row(i, half)])
        crecv[j, i, rows] += ptile[slot, core, pl.ds(0, n)]
        d, zj = lax.rem(j, 4), j // 4
        shift = jnp.where(d == 0, 4, jnp.where(d == 1, 3, jnp.where(d == 2, 5, 6)))
        target = lax.rem(x + shift, 4)
        distance = lax.rem(y - target + 4, 4)

        @pl.when(distance != 0)
        def _():
            remote(
                crecv.at[j, i, rows], yrecv.at[distance - 1, zj, i, rows],
                ysend, yrecv_sem.at[distance - 1, zj, sem_row(i, half)],
                (occ, zh * 8 + target * 2 + core),
            )

    def tiles(count, n, index, half=None, free=False):
        def step(k, _):
            @pl.when(k < n)
            def _():
                i, j = index(k)
                produce(i, j, half, lax.rem(count + k, SLOTS), free)

            @pl.when(k > 0)
            def _():
                i, j = index(k - 1)
                finish(i, j, half, lax.rem(count + k - 1, SLOTS))

            return 0

        lax.fori_loop(0, n + 1, step, 0)

    def settle(n):
        for slot in range(SLOTS):
            wait(ptile.at[slot, 0, pl.ds(0, n)], csend.at[slot])

    send_near("v", 0)
    send_near("v", 1)
    for half in range(2):
        spread(
            itg, itg_cols, None, half, x, vz.at[0, half],
            lambda a, b, half=half: remote(a, b, fsend.at[0, half], frecv.at[0, half], at(dzl=1)),
        )
    for half in range(2):
        spread(itg, itg_cols, None, half, x, stage.at[half], lambda a, b, half=half: pltpu.make_async_copy(a, b, own_sem.at[half]).start())
    for half in range(2):
        wait(stage.at[half], own_sem.at[half])
        split_v(stage.at[half], 0, half)
        spread(amp, amp_cols, amp_rows, half, x, stage.at[half], lambda a, b, half=half: pltpu.make_async_copy(a, b, own_sem.at[half]).start())
    for half in range(2):
        wait(stage.at[half], own_sem.at[half])
        split_a(stage.at[half], 0, half)

    take_v(0, 0)
    take_v(1, 0)
    send_near("a", 0)
    split_v(vx.at[0, 0], 1, 0)
    split_v(vx.at[1, 0], 2, 0)
    take_z(0, 0)

    take_v(0, 1)
    take_v(1, 1)
    send_near("a", 1)
    split_v(vx.at[0, 1], 1, 1)
    split_v(vx.at[1, 1], 2, 1)
    take_z(0, 1)
    tiles(0, 4, lambda k: (0, k + k // 3), free=True)

    take_a(0, 0)
    take_a(1, 0)
    send_far("v", 0)
    take_z(1, 0)

    take_a(0, 1)
    take_a(1, 1)
    send_far("v", 1)
    tiles(4, 4, lambda k: (1, k + k // 3), free=True)
    tiles(8, 4, lambda k: (2, k + k // 3))
    take_z(2, 0)

    take_v(2, 0)
    send_far("a", 0)
    split_v(vx.at[2, 0], 3, 0)
    take_z(1, 1)
    tiles(12, 3, lambda k: (k, 5))

    take_v(2, 1)
    send_far("a", 1)
    split_v(vx.at[2, 1], 3, 1)
    tiles(15, 3, lambda k: (k, 3))
    take_z(2, 1)
    tiles(18, 3, lambda k: (k, 6))

    mine = lax.rem(y - x + 4, 4)
    mine = jnp.where(mine == 0, 0, jnp.where(mine == 3, 1, jnp.where(mine == 1, 2, 3)))

    def collect(zj, i):
        for half in (None,) if i < 3 else (0, 1):
            for s in range(3):
                wait(yrecv.at[s, zj, i, rows_of(half)], yrecv_sem.at[s, zj, sem_row(i, half)])
        total[zj, i] = (crecv[zj * 4 + mine, i] + yrecv[0, zj, i]) + (yrecv[1, zj, i] + yrecv[2, zj, i])
        if i > 0:
            s = (None, 1, 0, 2)[i]
            remote(total.at[zj, i], xrecv.at[s, zj], osend.at[i - 1, zj], orecv.at[s, zj], at(dx=OFFSET[i]))

    take_a(2, 0)
    for i in (1, 2, 0):
        collect(0, i)
    take_z(3, 0)
    settle(ROWS)
    tiles(0, 7, lambda k: (3, k), half=0, free=True)

    take_a(2, 1)
    for slot in range(7):
        wait(ptile.at[slot, 0, pl.ds(0, HALF)], csend.at[slot])
    tiles(0, 7, lambda k: (3, k), half=1, free=True)
    collect(0, 3)
    take_z(3, 1)
    tiles(7, 1, lambda k: (3, 7), half=1, free=True)
    settle(HALF)
    tiles(0, 1, lambda k: (3, 7), half=0, free=True)
    tiles(1, 3, lambda k: (k, 7), free=True)
    for i in (3, 1, 2, 0):
        collect(1, i)
    wait(ptile.at[0, 0, pl.ds(0, HALF)], csend.at[0])
    for slot in (1, 2, 3):
        wait(ptile.at[slot, 0], csend.at[slot])

    keep = lax.rem(zl + zh, 2)
    for zj in range(2):
        for s in range(3):
            wait(xrecv.at[s, zj], orecv.at[s, zj])

    def summed(zj):
        return (total[zj, 0] + xrecv[0, zj]) + (xrecv[1, zj] + xrecv[2, zj])

    zsend[...] = summed(1 - keep)
    remote(zsend, zrecv, zsem.at[0], zsem.at[1], at(dzh=1))
    result = residual[...] + summed(keep)[: residual.shape[0]]
    wait(zrecv, zsem.at[1])
    out[...] = result + zrecv[: residual.shape[0]]

    wait(zsend, zsem.at[0])
    wait(yrecv, ysend)
    for s in range(3):
        for zj in range(2):
            wait(xrecv.at[s, zj], osend.at[s, zj])
        for half in range(2):
            wait(vx.at[s, half], gsend.at[s, half])
            wait(vx.at[s, half], gsend.at[s, 2 + half])
    for s in range(4):
        for half in range(2):
            wait(vz.at[s, half], fsend.at[s, half])


def body(integrals, amplitudes, residual_in):
    rows, columns = amplitudes.shape
    whole = columns // LANES * LANES
    itg_cols = jnp.pad(integrals[:, whole:], ((0, 0), (0, whole + LANES - columns)))
    amp_cols = jnp.pad(amplitudes[:, whole:], ((0, ROWS - rows), (0, whole + LANES - columns)))
    amp_rows = jnp.pad(amplitudes[ROWS - 8 :], ((0, ROWS - rows), (0, whole + LANES - columns)))
    any_spec = pl.BlockSpec(memory_space=pl.ANY)
    vmem_spec = pl.BlockSpec(memory_space=pltpu.VMEM)
    dma = pltpu.SemaphoreType.DMA
    return pl.pallas_call(
        kernel,
        name="ladder",
        out_shape=jax.ShapeDtypeStruct(residual_in.shape, F32),
        in_specs=[any_spec] * 5 + [vmem_spec],
        out_specs=vmem_spec,
        scratch_shapes=[
            pltpu.VMEM((3, 2, HALF, QUARTER), F32),
            pltpu.VMEM((4, 2, HALF, QUARTER), F32),
            pltpu.VMEM((3, ROWS, QUARTER), F32),
            pltpu.VMEM((2, HALF, QUARTER), F32),
            pltpu.VMEM((8, ROWS, QUARTER), BF16),
            pltpu.VMEM((8, ROWS, QUARTER), BF16),
            pltpu.VMEM((4, ROWS, QUARTER), BF16),
            pltpu.VMEM((4, ROWS, QUARTER), BF16),
            pltpu.VMEM((SLOTS, 2, ROWS, LANES), F32),
            pltpu.VMEM((8, 4, ROWS, LANES), F32),
            pltpu.VMEM((3, 2, 4, ROWS, LANES), F32),
            pltpu.VMEM((3, 2, ROWS, LANES), F32),
            pltpu.VMEM((2, 4, ROWS, LANES), F32),
            pltpu.VMEM((ROWS, LANES), F32),
            pltpu.VMEM((ROWS, LANES), F32),
            dma((2,)),
            dma((3, 4)),
            dma((3, 2)),
            dma((3, 2)),
            dma((4, 2)),
            dma((4, 2)),
            dma((SLOTS,)),
            dma((8, 5)),
            dma,
            dma((3, 2, 5)),
            dma((3, 2)),
            dma((3, 2)),
            dma((2,)),
        ],
        compiler_params=pltpu.CompilerParams(
            collective_id=0, has_side_effects=True, vmem_limit_bytes=60 * 2**20
        ),
        cost_estimate=pl.CostEstimate(flops=3 * 2 * 1008 * 2048 * 2048, bytes_accessed=2 * 2**24, transcendentals=0),
    )(amplitudes, amp_cols, amp_rows, integrals, itg_cols, residual_in)


def solution(mesh):
    return jax.shard_map(
        body,
        mesh=mesh,
        in_specs=(P("occ", "vir"), P("occ", "vir"), P("occ", "vir")),
        out_specs=P("occ", "vir"),
        check_vma=False,
    )
```

time: 534 us -> 260 us (0.49)
  the two profiles are of different devices: /device:TPU:32 before, /device:TPU:6 now
where the time goes in v1:
time: 260 us
  Pallas kernels  236 us (91%)
  local copies, waits for them, and re-layouts  24.2 us (9%)
    pallas_call x1, Pallas kernels, body(): pl.pallas_call(kernel, name='ladder', out_shape=jax.ShapeDtypeStruct(resi...  236 us
    unnamed x3, local copies, waits for them, and re-layouts  19.4 us

profile of v1, /device:TPU:6, one launch (start us, length us, event | category | flops | bytes accessed | tf_op | source)
XLA Modules:
  0.0 259.8 jit_solution(2424676151079537673)
XLA Ops:
  0.0 8.9 %copy.7.amp = f32[252,8176]{1,0:T(8,128)} copy(f32[252,8176]{0,1:T(8,128)} %param.4) | data formatting | bytes 16482816 | tf_op args[1]
  8.9 1.0 slice.13
  9.9 0.7 pad.13.amp_rows
  10.6 0.9 slice.12
  11.5 0.7 pad.12.amp_cols
  12.2 8.9 %copy.8.itg = f32[256,8176]{1,0:T(8,128)} copy(f32[256,8176]{0,1:T(8,128)} %param.3) | data formatting | bytes 16744448 | tf_op args[0]
  21.1 0.9 slice.14
  22.0 0.7 pad.14.itg_cols
  22.7 235.6 %ladder.1 = f32[252,128]{1,0:T(8,128)} custom-call(f32[252,8176]{1,0:T(8,128)} %copy.7.amp, f32[256,128]{1,0:T(8,128)} %pad.12.amp_cols, f32[8,8192]{1,0:T(8,128)} %pad.13.amp_rows, f32[256,8176]{1,0:T(8,128)} %copy.8.itg, f32[256,128]{1,0:T(8,128)} %pad.14.itg_cols, f32[252,128]{1,0:T(8,128)} %residual.1), custom_call_target="tpu_custom_call" | custom-call | flops 25367150592 | bytes 33554432 | tf_op jit(solution)/shard_map/ladder/pallas_call | solution.py:316
  258.3 1.6 copy.10

commit v2 on v1

v2 whole, which is shorter than its diff:
```python
import jax
import jax.numpy as jnp
from jax import lax
from jax.experimental import pallas as pl
from jax.experimental.pallas import tpu as pltpu
from jax.sharding import PartitionSpec as P

MESH = pl.DeviceIdType.MESH
F32, BF16 = jnp.float32, jnp.bfloat16

ROWS, HALF, LANES = 256, 128, 128
QUARTER, PART, UNIT, CHUNK = 2048, 1024, 512, 128
SHORT = 16
SLOTS = 8

OFFSET = (0, -1, 1, 2)


def dot(a, b):
    return jnp.dot(a, b, preferred_element_type=F32)


def kernel(
    amp, itg, residual, out, relay_v, relay_a,
    vx, vz, ax, afar, aside, stage_v, stage_a, vhi, vlo, ahi, alo, ptile, crecv, yrecv, xrecv, total, zsend, zrecv,
    own_v, own_a, gsend, grecv_v, grecv_a, hsend_v, hrecv_v, hsend_a, hrecv_a, rsend_v, rsend_a, far_recv, fsend, frecv, csend, crecv_sem, ysend, yrecv_sem,
    osend, orecv, zsem,
):
    occ, vir = lax.axis_index("occ"), lax.axis_index("vir")
    x, zl = lax.rem(occ, 4), occ // 4
    core, y, zh = lax.rem(vir, 2), lax.rem(vir // 2, 4), vir // 8

    def at(dx=0, dzl=0, dy=0, dzh=0, dc=0):
        return (
            lax.rem(zl + dzl, 2) * 4 + lax.rem(x + dx + 4, 4),
            lax.rem(zh + dzh, 2) * 8 + lax.rem(y + dy + 4, 4) * 2 + lax.rem(core + dc, 2),
        )

    peers = [at(dx=1), at(dx=-1), at(dx=2), at(dzl=1), at(dc=1), at(dy=1), at(dy=-1), at(dy=2), at(dzh=1)]
    barrier = pltpu.get_barrier_semaphore()
    for peer in peers:
        pl.semaphore_signal(barrier, inc=1, device_id=peer, device_id_type=MESH)
    pl.semaphore_wait(barrier, len(peers))

    def remote(src, dst, ssem, rsem, device):
        pltpu.make_async_remote_copy(
            src_ref=src, dst_ref=dst, send_sem=ssem, recv_sem=rsem, device_id=device, device_id_type=MESH
        ).start()

    def wait(ref, sem):
        pltpu.make_async_copy(ref, ref, sem).wait()

    def sized(start, size, quarter, act):
        if start + size < QUARTER:
            act(pl.ds(start, size), pl.ds(pl.multiple_of(quarter * QUARTER + start, SHORT), size))
        else:

            @pl.when(quarter != 3)
            def _():
                act(pl.ds(start, size), pl.ds(pl.multiple_of(quarter * QUARTER + start, SHORT), size))

            @pl.when(quarter == 3)
            def _():
                act(pl.ds(start, size - SHORT), pl.ds(3 * QUARTER + start, size - SHORT))

    def quarter_of(dx):
        return lax.rem(x + dx + 4, 4)

    def send(kind, half, dx, s):
        device = at(dx=dx)

        def act(local, whole):
            if kind == "v":
                remote(itg.at[whole], vx.at[s, local], gsend.at[s, half], grecv_v.at[s, half], device)
            else:
                remote(amp.at[whole], ax.at[s, local], gsend.at[s, 2 + half], grecv_a.at[s, half], device)

        sized(half * PART, PART, quarter_of(dx), act)

    def send_near(kind, half):
        send(kind, half, 1, 0)
        send(kind, half, -1, 1)

    def via(way):
        return at(dx=1 - 2 * way)

    def start_v(way):
        def act(local, whole):
            dst = relay_v.at[way, pl.ds(0, local.size)]
            remote(itg.at[whole], dst, hsend_v.at[way], hrecv_v.at[way], via(way))

        sized(way * PART, PART, quarter_of(2), act)

    def pass_v(way):
        def act(local, _):
            src = relay_v.at[way, pl.ds(0, local.size)]
            wait(src, hrecv_v.at[way])
            remote(src, vx.at[2, local], rsend_v.at[way], grecv_v.at[2, way], via(way))

        sized(way * PART, PART, quarter_of(1 - 2 * way), act)

    def start_a(side, way):
        def act(local, whole):
            src = amp.at[whole, pl.ds(0, HALF)] if side == 0 else aside.at[local]
            dst = relay_a.at[side, way, pl.ds(0, local.size)]
            remote(src, dst, hsend_a.at[side, way], hrecv_a.at[side, way], via(way))

        sized(way * PART, PART, quarter_of(2), act)

    def pass_a(side, way):
        def act(local, _):
            src = relay_a.at[side, way, pl.ds(0, local.size)]
            wait(src, hrecv_a.at[side, way])
            remote(src, afar.at[side, local], rsend_a.at[side, way], far_recv.at[side, way], via(way))

        sized(way * PART, PART, quarter_of(1 - 2 * way), act)

    def forward(s, half):
        rows = pl.ds(half * PART, PART)
        remote(vx.at[s, rows], vz.at[s + 1, rows], fsend.at[s + 1, half], frecv.at[s + 1, half], at(dzl=1))

    limit = jnp.where(x == 3, QUARTER - SHORT, QUARTER)

    def known(value, start):
        index = lax.broadcasted_iota(jnp.int32, value.shape, 0) + start
        return jnp.where(index < limit, value, 0.0)

    def split_v(src, j, start, size):
        def step(c, _):
            at_row = pl.multiple_of(c * CHUNK, CHUNK)
            value = known(src[pl.ds(at_row, CHUNK)], start + at_row)
            high = value.astype(BF16)
            rows = pl.ds(pl.multiple_of(start + at_row, CHUNK), CHUNK)
            vhi[j, rows] = high
            vlo[j, rows] = (value - high.astype(F32)).astype(BF16)
            return 0

        lax.fori_loop(0, size // CHUNK, step, 0)

    def split_a(src, i, row0, start, size):
        rows = pl.ds(row0, src.shape[1])

        def step(c, _):
            at_row = pl.multiple_of(c * CHUNK, CHUNK)
            value = known(src[pl.ds(at_row, CHUNK)], start + at_row).T
            high = value.astype(BF16)
            columns = pl.ds(pl.multiple_of(start + at_row, CHUNK), CHUNK)
            ahi[i, rows, columns] = high
            alo[i, rows, columns] = (value - high.astype(F32)).astype(BF16)
            return 0

        lax.fori_loop(0, size // CHUNK, step, 0)

    def take_v(s, half):
        sized(half * PART, PART, x, lambda local, _: wait(vx.at[s, local], grecv_v.at[s, half]))
        forward(s, half)

    def split_taken(s, half):
        split_v(vx.at[s, pl.ds(half * PART, PART)], s + 1, half * PART, PART)

    def take_z(s, half):
        rows = pl.ds(half * PART, PART)
        if s == 0:
            sized(half * PART, PART, x, lambda local, _: wait(vz.at[s, local], frecv.at[s, half]))
        else:
            wait(vz.at[s, rows], frecv.at[s, half])
        split_v(vz.at[s, rows], 4 + s, half * PART, PART)

    def take_a(s, half):
        sized(half * PART, PART, x, lambda local, _: wait(ax.at[s, local], grecv_a.at[s, half]))
        split_a(ax.at[s, pl.ds(half * PART, PART)], s + 1, 0, half * PART, PART)

    def take_far(side):
        for way in range(2):
            sized(way * PART, PART, x, lambda local, _: wait(afar.at[side, local], far_recv.at[side, way]))
        split_a(afar.at[side], 3, side * HALF, 0, QUARTER)

    def load_v(u, act):
        sized(u * UNIT, UNIT, x, lambda local, whole: act(
            itg.at[whole], stage_v.at[u % 2, pl.ds(0, local.size)], own_v.at[u % 2]))

    def load_a(u, act):
        sized(u % 4 * UNIT, UNIT, x if u < 4 else quarter_of(2), lambda local, whole: act(
            amp.at[whole], stage_a.at[u % 2, pl.ds(0, local.size)], own_a.at[u % 2]))

    def begin(src, dst, sem):
        pltpu.make_async_copy(src, dst, sem).start()

    def end(src, dst, sem):
        wait(dst, sem)

    def set_aside(u):
        def step(c, _):
            at_row = pl.multiple_of(c * CHUNK, CHUNK)
            n = amp.shape[1] - HALF
            aside[pl.ds(pl.multiple_of(u % 4 * UNIT + at_row, CHUNK), CHUNK), pl.ds(0, n)] = stage_a[
                u % 2, pl.ds(at_row, CHUNK), pl.ds(HALF, n)
            ]
            return 0

        lax.fori_loop(0, UNIT // CHUNK, step, 0)

    def rows_of(half):
        return pl.ds(0, ROWS) if half is None else pl.ds(half * HALF, HALF)

    def sem_row(i, half):
        return i if half is None else 3 + half

    def produce(i, j, half, slot, free):
        rows = rows_of(half)
        n = ROWS if half is None else HALF
        if not free:
            wait(ptile.at[slot, 0, pl.ds(0, n)], csend.at[slot])
        high, low = ahi[i, rows], alo[i, rows]
        both = jnp.concatenate([high, low], axis=0)
        one = dot(both, vhi[j])
        if half is None:
            value = one[:n] + one[n:] + dot(high, vlo[j])
        else:
            two = dot(both, vlo[j])
            value = one[:n] + one[n:] + two[:n] + two[n:]
        ptile[slot, 0, pl.ds(0, n)] = value[:, :LANES]
        ptile[slot, 1, pl.ds(0, n)] = value[:, LANES:]
        remote(
            ptile.at[slot, 1 - core, pl.ds(0, n)], crecv.at[j, i, rows],
            csend.at[slot], crecv_sem.at[j, sem_row(i, half)], at(dc=1),
        )

    def finish(i, j, half, slot):
        rows = rows_of(half)
        n = ROWS if half is None else HALF
        wait(crecv.at[j, i, rows], crecv_sem.at[j, sem_row(i, half)])
        crecv[j, i, rows] += ptile[slot, core, pl.ds(0, n)]
        d, zj = lax.rem(j, 4), j // 4
        shift = jnp.where(d == 0, 4, jnp.where(d == 1, 3, jnp.where(d == 2, 5, 6)))
        target = lax.rem(x + shift, 4)
        distance = lax.rem(y - target + 4, 4)

        @pl.when(distance != 0)
        def _():
            remote(
                crecv.at[j, i, rows], yrecv.at[distance - 1, zj, i, rows],
                ysend, yrecv_sem.at[distance - 1, zj, sem_row(i, half)],
                (occ, zh * 8 + target * 2 + core),
            )

    def tiles(count, n, index, half=None, free=False):
        def step(k, _):
            @pl.when(k < n)
            def _():
                i, j = index(k)
                produce(i, j, half, lax.rem(count + k, SLOTS), free)

            @pl.when(k > 0)
            def _():
                i, j = index(k - 1)
                finish(i, j, half, lax.rem(count + k - 1, SLOTS))

            return 0

        lax.fori_loop(0, n + 1, step, 0)

    def settle(n):
        for slot in range(SLOTS):
            wait(ptile.at[slot, 0, pl.ds(0, n)], csend.at[slot])

    for half in range(2):
        send_near("v", half)
        sized(half * PART, PART, x, lambda local, whole, half=half: remote(
            itg.at[whole], vz.at[0, local], fsend.at[0, half], frecv.at[0, half], at(dzl=1)))
    send_near("a", 0)
    for way in range(2):
        start_v(way)
    send_near("a", 1)
    for u in range(2):
        load_v(u, begin)
        load_a(u, begin)
    for u in range(4):
        load_v(u, end)
        split_v(stage_v.at[u % 2], 0, u * UNIT, UNIT)
        if u < 2:
            load_v(u + 2, begin)
    for u in range(8):
        load_a(u, end)
        if u < 4:
            split_a(stage_a.at[u % 2], 0, 0, u * UNIT, UNIT)
        else:
            set_aside(u)
        if u < 6:
            load_a(u + 2, begin)

    take_v(0, 0)
    take_v(1, 0)
    split_taken(0, 0)
    split_taken(1, 0)
    take_z(0, 0)

    take_v(0, 1)
    take_v(1, 1)
    split_taken(0, 1)
    split_taken(1, 1)
    take_z(0, 1)
    tiles(0, 4, lambda k: (0, k + k // 3), free=True)

    take_a(0, 0)
    take_a(1, 0)
    take_z(1, 0)

    for way in range(2):
        pass_v(way)
    for side in range(2):
        for way in range(2):
            start_a(side, way)
    take_z(2, 0)

    take_a(0, 1)
    take_a(1, 1)
    tiles(4, 4, lambda k: (1, k + k // 3), free=True)
    tiles(8, 4, lambda k: (2, k + k // 3))
    take_z(1, 1)
    tiles(12, 3, lambda k: (k, 5))

    take_v(2, 0)
    take_v(2, 1)
    split_taken(2, 0)
    split_taken(2, 1)
    tiles(15, 3, lambda k: (k, 3))
    take_z(2, 1)
    tiles(18, 3, lambda k: (k, 6))

    mine = lax.rem(y - x + 4, 4)
    mine = jnp.where(mine == 0, 0, jnp.where(mine == 3, 1, jnp.where(mine == 1, 2, 3)))

    def collect(zj, i):
        for half in (None,) if i < 3 else (0, 1):
            for s in range(3):
                wait(yrecv.at[s, zj, i, rows_of(half)], yrecv_sem.at[s, zj, sem_row(i, half)])
        total[zj, i] = (crecv[zj * 4 + mine, i] + yrecv[0, zj, i]) + (yrecv[1, zj, i] + yrecv[2, zj, i])
        if i > 0:
            s = (None, 1, 0, 2)[i]
            remote(total.at[zj, i], xrecv.at[s, zj], osend.at[i - 1, zj], orecv.at[s, zj], at(dx=OFFSET[i]))

    for way in range(2):
        pass_a(0, way)
    for i in (1, 2, 0):
        collect(0, i)
    for way in range(2):
        pass_a(1, way)
    take_z(3, 0)
    take_far(0)
    settle(ROWS)
    tiles(0, 7, lambda k: (3, k), half=0, free=True)

    take_far(1)
    for slot in range(7):
        wait(ptile.at[slot, 0, pl.ds(0, HALF)], csend.at[slot])
    tiles(0, 7, lambda k: (3, k), half=1, free=True)
    collect(0, 3)
    take_z(3, 1)
    tiles(7, 1, lambda k: (3, 7), half=1, free=True)
    settle(HALF)
    tiles(0, 1, lambda k: (3, 7), half=0, free=True)
    tiles(1, 3, lambda k: (k, 7), free=True)
    for i in (3, 1, 2, 0):
        collect(1, i)
    wait(ptile.at[0, 0, pl.ds(0, HALF)], csend.at[0])
    for slot in (1, 2, 3):
        wait(ptile.at[slot, 0], csend.at[slot])

    keep = lax.rem(zl + zh, 2)
    for zj in range(2):
        for s in range(3):
            wait(xrecv.at[s, zj], orecv.at[s, zj])

    def summed(zj):
        return (total[zj, 0] + xrecv[0, zj]) + (xrecv[1, zj] + xrecv[2, zj])

    zsend[...] = summed(1 - keep)
    remote(zsend, zrecv, zsem.at[0], zsem.at[1], at(dzh=1))
    result = residual[...] + summed(keep)[: residual.shape[0]]
    wait(zrecv, zsem.at[1])
    out[...] = result + zrecv[: residual.shape[0]]

    wait(zsend, zsem.at[0])
    wait(yrecv, ysend)
    for s in range(3):
        for zj in range(2):
            wait(xrecv.at[s, zj], osend.at[s, zj])
    for half in range(2):
        for s, dx in enumerate((1, -1)):
            sized(half * PART, PART, quarter_of(dx), lambda local, _: wait(vx.at[s, local], gsend.at[s, half]))
            sized(half * PART, PART, quarter_of(dx), lambda local, _: wait(ax.at[s, local], gsend.at[s, 2 + half]))
        way = half
        sized(way * PART, PART, quarter_of(2), lambda local, _: wait(vx.at[2, local], hsend_v.at[way]))
        sized(way * PART, PART, quarter_of(1 - 2 * way), lambda local, _: wait(vx.at[2, local], rsend_v.at[way]))
        for side in range(2):
            sized(way * PART, PART, quarter_of(2), lambda local, _: wait(afar.at[side, local], hsend_a.at[side, way]))
            sized(way * PART, PART, quarter_of(1 - 2 * way), lambda local, _: wait(afar.at[side, local], rsend_a.at[side, way]))
    for half in range(2):
        sized(half * PART, PART, x, lambda local, _: wait(vz.at[0, local], fsend.at[0, half]))
        for s in range(1, 4):
            wait(vz.at[s, pl.ds(half * PART, PART)], fsend.at[s, half])


def body(integrals, amplitudes, residual_in):
    rows = amplitudes.shape[0]
    any_spec = pl.BlockSpec(memory_space=pl.ANY)
    vmem_spec = pl.BlockSpec(memory_space=pltpu.VMEM)
    dma = pltpu.SemaphoreType.DMA
    return pl.pallas_call(
        kernel,
        name="ladder",
        out_shape=(
            jax.ShapeDtypeStruct(residual_in.shape, F32),
            jax.ShapeDtypeStruct((2, PART, ROWS), F32),
            jax.ShapeDtypeStruct((2, 2, PART, HALF), F32),
        ),
        in_specs=[any_spec] * 2 + [vmem_spec],
        out_specs=(vmem_spec, any_spec, any_spec),
        scratch_shapes=[
            pltpu.VMEM((3, QUARTER, ROWS), F32),
            pltpu.VMEM((4, QUARTER, ROWS), F32),
            pltpu.VMEM((2, QUARTER, rows), F32),
            pltpu.VMEM((2, QUARTER, HALF), F32),
            pltpu.VMEM((QUARTER, HALF), F32),
            pltpu.VMEM((2, UNIT, ROWS), F32),
            pltpu.VMEM((2, UNIT, rows), F32),
            pltpu.VMEM((8, QUARTER, ROWS), BF16),
            pltpu.VMEM((8, QUARTER, ROWS), BF16),
            pltpu.VMEM((4, ROWS, QUARTER), BF16),
            pltpu.VMEM((4, ROWS, QUARTER), BF16),
            pltpu.VMEM((SLOTS, 2, ROWS, LANES), F32),
            pltpu.VMEM((8, 4, ROWS, LANES), F32),
            pltpu.VMEM((3, 2, 4, ROWS, LANES), F32),
            pltpu.VMEM((3, 2, ROWS, LANES), F32),
            pltpu.VMEM((2, 4, ROWS, LANES), F32),
            pltpu.VMEM((ROWS, LANES), F32),
            pltpu.VMEM((ROWS, LANES), F32),
            dma((2,)),
            dma((2,)),
            dma((2, 4)),
            dma((3, 2)),
            dma((2, 2)),
            dma((2,)),
            dma((2,)),
            dma((2, 2)),
            dma((2, 2)),
            dma((2,)),
            dma((2, 2)),
            dma((2, 2)),
            dma((4, 2)),
            dma((4, 2)),
            dma((SLOTS,)),
            dma((8, 5)),
            dma,
            dma((3, 2, 5)),
            dma((3, 2)),
            dma((3, 2)),
            dma((2,)),
        ],
        compiler_params=pltpu.CompilerParams(
            collective_id=0, has_side_effects=True, vmem_limit_bytes=61 * 2**20
        ),
        cost_estimate=pl.CostEstimate(flops=3 * 2 * 1008 * 2048 * 2048, bytes_accessed=2 * 2**24, transcendentals=0),
    )(amplitudes.T, integrals.T, residual_in)[0]


def solution(mesh):
    return jax.shard_map(
        body,
        mesh=mesh,
        in_specs=(P("occ", "vir"), P("occ", "vir"), P("occ", "vir")),
        out_specs=P("occ", "vir"),
        check_vma=False,
    )
```

time: 260 us -> 240 us (0.923)
  local copies, waits for them, and re-layouts: 24.2 us -> 1.57 us
    unnamed x3 -> x1, local copies, waits for them, and re-layouts: 19.4 us -> 1.57 us
    slice x3 -> x0, local copies, waits for them, and re-layouts: 2.79 us -> none  [the longest x1 0.97 us: body(): amplitudes[ROWS - 8:]]
    pallas_call x1, Pallas kernels: 236 us -> 238 us  [body(): pl.pallas_call(kernel, name='ladder', out_shape=(jax.ShapeDtypeStruct(res...]
where the time goes in v2:
time: 240 us
  Pallas kernels  238 us (99%)
    pallas_call x1, Pallas kernels, body(): pl.pallas_call(kernel, name='ladder', out_shape=(jax.ShapeDtypeStruct(res...  238 us

profile of v2, /device:TPU:6, one launch (start us, length us, event | category | flops | bytes accessed | tf_op | source)
XLA Modules:
  0.0 239.9 jit_solution(6231573699935488195)
XLA Ops:
  0.0 238.3 %ladder.1 = (f32[252,128]{1,0:T(8,128)}, f32[2,1024,256]{2,1,0:T(8,128)}, f32[2,2,1024,128]{3,2,1,0:T(8,128)}) custom-call(f32[8176,252]{1,0:T(8,128)} %bitcast.2, f32[8176,256]{1,0:T(8,128)} %bitcast.3, f32[252,128]{1,0:T(8,128)} %residual.1), custom_call_target="tpu_custom_call" | custom-call | flops 25367150592 | bytes 33554432 | tf_op jit(solution)/shard_map/ladder/pallas_call | solution.py:410
  238.3 1.6 copy.5

commit v3 on v2

--- a/solution.py
+++ b/solution.py
@@ -11,7 +11,7 @@
 ROWS, HALF, LANES = 256, 128, 128
 QUARTER, PART, UNIT, CHUNK = 2048, 1024, 512, 128
 SHORT = 16
-SLOTS = 8
+SLOTS = 4
 
 OFFSET = (0, -1, 1, 2)
 
@@ -21,9 +21,9 @@
 
 
 def kernel(
-    amp, itg, residual, out, relay_v, relay_a,
-    vx, vz, ax, afar, aside, stage_v, stage_a, vhi, vlo, ahi, alo, ptile, crecv, yrecv, xrecv, total, zsend, zrecv,
-    own_v, own_a, gsend, grecv_v, grecv_a, hsend_v, hrecv_v, hsend_a, hrecv_a, rsend_v, rsend_a, far_recv, fsend, frecv, csend, crecv_sem, ysend, yrecv_sem,
+    amp, itg, out, relay_v, relay_a,
+    vx, vz, ax, afar, aside, stage_v, stage_a, vhi, vlo, ahi, alo, ptile, plast, crecv, yrecv, xrecv, total, zsend, zrecv,
+    own_v, own_a, gsend, grecv_v, grecv_a, hsend_v, hrecv_v, hsend_a, hrecv_a, rsend_v, rsend_a, far_recv, fsend, frecv, csend, lsend, crecv_sem, ysend, yrecv_sem,
     osend, orecv, zsem,
 ):
     occ, vir = lax.axis_index("occ"), lax.axis_index("vir")
@@ -125,14 +125,14 @@
         index = lax.broadcasted_iota(jnp.int32, value.shape, 0) + start
         return jnp.where(index < limit, value, 0.0)
 
-    def split_v(src, j, start, size):
+    def split_v(src, j, start, size, lanes=pl.ds(0, ROWS)):
         def step(c, _):
             at_row = pl.multiple_of(c * CHUNK, CHUNK)
             value = known(src[pl.ds(at_row, CHUNK)], start + at_row)
             high = value.astype(BF16)
             rows = pl.ds(pl.multiple_of(start + at_row, CHUNK), CHUNK)
-            vhi[j, rows] = high
-            vlo[j, rows] = (value - high.astype(F32)).astype(BF16)
+            vhi[j, rows, lanes] = high
+            vlo[j, rows, lanes] = (value - high.astype(F32)).astype(BF16)
             return 0
 
         lax.fori_loop(0, size // CHUNK, step, 0)
@@ -153,7 +153,17 @@
 
     def take_v(s, half):
         sized(half * PART, PART, x, lambda local, _: wait(vx.at[s, local], grecv_v.at[s, half]))
-        forward(s, half)
+        if s < 2:
+            forward(s, half)
+
+    def forward_last(side):
+        lanes = pl.ds(side * LANES, LANES)
+        remote(vx.at[2, :, lanes], vz.at[3, :, lanes], fsend.at[3, side], frecv.at[3, side], at(dzl=1))
+
+    def take_last(side):
+        lanes = pl.ds(side * LANES, LANES)
+        wait(vz.at[3, :, lanes], frecv.at[3, side])
+        split_v(vz.at[3, :, lanes], 7, 0, QUARTER, lanes)
 
     def split_taken(s, half):
         split_v(vx.at[s, pl.ds(half * PART, PART)], s + 1, half * PART, PART)
@@ -206,19 +216,19 @@
     def sem_row(i, half):
         return i if half is None else 3 + half
 
-    def produce(i, j, half, slot, free):
+    def product(i, rows, n, high_v, low_v):
+        high, low = ahi[i, rows], alo[i, rows]
+        both = jnp.concatenate([high, low], axis=0)
+        one = dot(both, high_v)
+        if n == ROWS:
+            return one[:n] + one[n:] + dot(high, low_v)
+        two = dot(both, low_v)
+        return one[:n] + one[n:] + two[:n] + two[n:]
+
+    def produce(i, j, half, slot):
         rows = rows_of(half)
         n = ROWS if half is None else HALF
-        if not free:
-            wait(ptile.at[slot, 0, pl.ds(0, n)], csend.at[slot])
-        high, low = ahi[i, rows], alo[i, rows]
-        both = jnp.concatenate([high, low], axis=0)
-        one = dot(both, vhi[j])
-        if half is None:
-            value = one[:n] + one[n:] + dot(high, vlo[j])
-        else:
-            two = dot(both, vlo[j])
-            value = one[:n] + one[n:] + two[:n] + two[n:]
+        value = product(i, rows, n, vhi[j], vlo[j])
         ptile[slot, 0, pl.ds(0, n)] = value[:, :LANES]
         ptile[slot, 1, pl.ds(0, n)] = value[:, LANES:]
         remote(
@@ -226,11 +236,11 @@
             csend.at[slot], crecv_sem.at[j, sem_row(i, half)], at(dc=1),
         )
 
-    def finish(i, j, half, slot):
+    def finish(i, j, half, own):
         rows = rows_of(half)
         n = ROWS if half is None else HALF
         wait(crecv.at[j, i, rows], crecv_sem.at[j, sem_row(i, half)])
-        crecv[j, i, rows] += ptile[slot, core, pl.ds(0, n)]
+        crecv[j, i, rows] += own[pl.ds(0, n)]
         d, zj = lax.rem(j, 4), j // 4
         shift = jnp.where(d == 0, 4, jnp.where(d == 1, 3, jnp.where(d == 2, 5, 6)))
         target = lax.rem(x + shift, 4)
@@ -244,17 +254,23 @@
                 (occ, zh * 8 + target * 2 + core),
             )
 
-    def tiles(count, n, index, half=None, free=False):
+    def tiles(count, n, index, half=None, free=0):
         def step(k, _):
             @pl.when(k < n)
             def _():
                 i, j = index(k)
-                produce(i, j, half, lax.rem(count + k, SLOTS), free)
+                slot = lax.rem(count + k, SLOTS)
+
+                @pl.when(k >= free)
+                def _():
+                    wait(ptile.at[slot, 0, pl.ds(0, ROWS if half is None else HALF)], csend.at[slot])
+
+                produce(i, j, half, slot)
 
             @pl.when(k > 0)
             def _():
                 i, j = index(k - 1)
-                finish(i, j, half, lax.rem(count + k - 1, SLOTS))
+                finish(i, j, half, ptile.at[lax.rem(count + k - 1, SLOTS), core])
 
             return 0
 
@@ -263,6 +279,33 @@
     def settle(n):
         for slot in range(SLOTS):
             wait(ptile.at[slot, 0, pl.ds(0, n)], csend.at[slot])
+
+    def last_tiles(side, n, half=None):
+        lanes = pl.ds(side * LANES, LANES)
+        rows = rows_of(half)
+        block = (lambda k: k) if half is None else (lambda k: 3)
+
+        def step(k, _):
+            @pl.when(k < n)
+            def _():
+                i = block(k)
+                plast[side, i, rows] = product(i, rows, ROWS if half is None else HALF, vhi[7, :, lanes], vlo[7, :, lanes])
+
+                @pl.when(core != side)
+                def _():
+                    remote(
+                        plast.at[side, i, rows], crecv.at[7, i, rows],
+                        lsend.at[side, sem_row(i, half)], crecv_sem.at[7, sem_row(i, half)], at(dc=1),
+                    )
+
+            @pl.when((k > 0) & (core == side))
+            def _():
+                i = block(k - 1)
+                finish(i, 7, half, plast.at[side, i, rows])
+
+            return 0
+
+        lax.fori_loop(0, n + 1, step, 0)
 
     for half in range(2):
         send_near("v", half)
@@ -300,7 +343,7 @@
     split_taken(0, 1)
     split_taken(1, 1)
     take_z(0, 1)
-    tiles(0, 4, lambda k: (0, k + k // 3), free=True)
+    tiles(0, 4, lambda k: (0, k + k // 3), free=4)
 
     take_a(0, 0)
     take_a(1, 0)
@@ -315,13 +358,14 @@
 
     take_a(0, 1)
     take_a(1, 1)
-    tiles(4, 4, lambda k: (1, k + k // 3), free=True)
-    tiles(8, 4, lambda k: (2, k + k // 3))
+    tiles(4, 8, lambda k: (1 + k // 4, k % 4 + k % 4 // 3))
     take_z(1, 1)
     tiles(12, 3, lambda k: (k, 5))
 
     take_v(2, 0)
     take_v(2, 1)
+    forward_last(0)
+    forward_last(1)
     split_taken(2, 0)
     split_taken(2, 1)
     tiles(15, 3, lambda k: (k, 3))
@@ -331,61 +375,105 @@
     mine = lax.rem(y - x + 4, 4)
     mine = jnp.where(mine == 0, 0, jnp.where(mine == 3, 1, jnp.where(mine == 1, 2, 3)))
 
-    def collect(zj, i):
-        for half in (None,) if i < 3 else (0, 1):
-            for s in range(3):
-                wait(yrecv.at[s, zj, i, rows_of(half)], yrecv_sem.at[s, zj, sem_row(i, half)])
-        total[zj, i] = (crecv[zj * 4 + mine, i] + yrecv[0, zj, i]) + (yrecv[1, zj, i] + yrecv[2, zj, i])
+    def collect(zj, i, half=None):
+        row = sem_row(i, half)
+        start = 0 if half is None else half * HALF
+        for s in range(3):
+            wait(yrecv.at[s, zj, i, rows_of(half)], yrecv_sem.at[s, zj, row])
+
+        def step(c, _):
+            rows = pl.ds(pl.multiple_of(start + c * 32, 32), 32)
+            total[zj, i, rows] = (crecv[zj * 4 + mine, i, rows] + yrecv[0, zj, i, rows]) + (
+                yrecv[1, zj, i, rows] + yrecv[2, zj, i, rows]
+            )
+            return 0
+
+        lax.fori_loop(0, (ROWS if half is None else HALF) // 32, step, 0)
         if i > 0:
-            s = (None, 1, 0, 2)[i]
-            remote(total.at[zj, i], xrecv.at[s, zj], osend.at[i - 1, zj], orecv.at[s, zj], at(dx=OFFSET[i]))
+            s, rows = (None, 1, 0, 2)[i], rows_of(half)
+            remote(
+                total.at[zj, i, rows], xrecv.at[s, zj, rows],
+                osend.at[row - 1, zj], orecv.at[row - 1, zj], at(dx=OFFSET[i]),
+            )
+
+    late = mine == 3
 
     for way in range(2):
         pass_a(0, way)
     for i in (1, 2, 0):
         collect(0, i)
+
+    @pl.when(~late)
+    def _():
+        for i in (1, 2, 0):
+            collect(1, i)
+
     for way in range(2):
         pass_a(1, way)
-    take_z(3, 0)
+    take_last(0)
+    last_tiles(0, 3)
     take_far(0)
     settle(ROWS)
-    tiles(0, 7, lambda k: (3, k), half=0, free=True)
-
+    tiles(0, 7, lambda k: (3, k), half=0, free=SLOTS)
+    last_tiles(0, 1, half=0)
+    collect(0, 3, 0)
+
+    @pl.when(~late)
+    def _():
+        collect(1, 3, 0)
+
+    @pl.when(late & (core == 0))
+    def _():
+        for i in (1, 2, 0):
+            collect(1, i)
+        collect(1, 3, 0)
+
+    settle(HALF)
+    take_last(1)
+    last_tiles(1, 3)
+    last_tiles(1, 1, half=0)
     take_far(1)
-    for slot in range(7):
-        wait(ptile.at[slot, 0, pl.ds(0, HALF)], csend.at[slot])
-    tiles(0, 7, lambda k: (3, k), half=1, free=True)
-    collect(0, 3)
-    take_z(3, 1)
-    tiles(7, 1, lambda k: (3, 7), half=1, free=True)
-    settle(HALF)
-    tiles(0, 1, lambda k: (3, 7), half=0, free=True)
-    tiles(1, 3, lambda k: (k, 7), free=True)
-    for i in (3, 1, 2, 0):
-        collect(1, i)
-    wait(ptile.at[0, 0, pl.ds(0, HALF)], csend.at[0])
-    for slot in (1, 2, 3):
-        wait(ptile.at[slot, 0], csend.at[slot])
+    tiles(0, 7, lambda k: (3, k), half=1, free=SLOTS)
+    last_tiles(0, 1, half=1)
+    last_tiles(1, 1, half=1)
+
+    @pl.when(late & (core == 1))
+    def _():
+        for i in (1, 2, 0):
+            collect(1, i)
+        collect(1, 3, 0)
+
+    collect(0, 3, 1)
+    collect(1, 3, 1)
 
     keep = lax.rem(zl + zh, 2)
+    parts = [(i, None) for i in (1, 2)] + [(3, half) for half in range(2)]
     for zj in range(2):
-        for s in range(3):
-            wait(xrecv.at[s, zj], orecv.at[s, zj])
+        for i, half in parts:
+            wait(xrecv.at[(None, 1, 0, 2)[i], zj, rows_of(half)], orecv.at[sem_row(i, half) - 1, zj])
 
     def summed(zj):
         return (total[zj, 0] + xrecv[0, zj]) + (xrecv[1, zj] + xrecv[2, zj])
 
     zsend[...] = summed(1 - keep)
     remote(zsend, zrecv, zsem.at[0], zsem.at[1], at(dzh=1))
-    result = residual[...] + summed(keep)[: residual.shape[0]]
+    result = summed(keep)[: out.shape[0]]
     wait(zrecv, zsem.at[1])
-    out[...] = result + zrecv[: residual.shape[0]]
+    out[...] = result + zrecv[: out.shape[0]]
 
     wait(zsend, zsem.at[0])
     wait(yrecv, ysend)
-    for s in range(3):
-        for zj in range(2):
-            wait(xrecv.at[s, zj], osend.at[s, zj])
+    settle(HALF)
+    for zj in range(2):
+        for i, half in parts:
+            wait(total.at[zj, i, rows_of(half)], osend.at[sem_row(i, half) - 1, zj])
+    for side in range(2):
+
+        @pl.when(core != side)
+        def _():
+            for i, half in [(0, None)] + parts:
+                wait(plast.at[side, i, rows_of(half)], lsend.at[side, sem_row(i, half)])
+
     for half in range(2):
         for s, dx in enumerate((1, -1)):
             sized(half * PART, PART, quarter_of(dx), lambda local, _: wait(vx.at[s, local], gsend.at[s, half]))
@@ -407,7 +495,7 @@
     any_spec = pl.BlockSpec(memory_space=pl.ANY)
     vmem_spec = pl.BlockSpec(memory_space=pltpu.VMEM)
     dma = pltpu.SemaphoreType.DMA
-    return pl.pallas_call(
+    ladder = pl.pallas_call(
         kernel,
         name="ladder",
         out_shape=(
@@ -415,7 +503,7 @@
             jax.ShapeDtypeStruct((2, PART, ROWS), F32),
             jax.ShapeDtypeStruct((2, 2, PART, HALF), F32),
         ),
-        in_specs=[any_spec] * 2 + [vmem_spec],
+        in_specs=[any_spec] * 2,
         out_specs=(vmem_spec, any_spec, any_spec),
         scratch_shapes=[
             pltpu.VMEM((3, QUARTER, ROWS), F32),
@@ -430,6 +518,7 @@
             pltpu.VMEM((4, ROWS, QUARTER), BF16),
             pltpu.VMEM((4, ROWS, QUARTER), BF16),
             pltpu.VMEM((SLOTS, 2, ROWS, LANES), F32),
+            pltpu.VMEM((2, 4, ROWS, LANES), F32),
             pltpu.VMEM((8, 4, ROWS, LANES), F32),
             pltpu.VMEM((3, 2, 4, ROWS, LANES), F32),
             pltpu.VMEM((3, 2, ROWS, LANES), F32),
@@ -451,18 +540,20 @@
             dma((4, 2)),
             dma((4, 2)),
             dma((SLOTS,)),
+            dma((2, 5)),
             dma((8, 5)),
             dma,
             dma((3, 2, 5)),
-            dma((3, 2)),
-            dma((3, 2)),
+            dma((4, 2)),
+            dma((4, 2)),
             dma((2,)),
         ],
         compiler_params=pltpu.CompilerParams(
             collective_id=0, has_side_effects=True, vmem_limit_bytes=61 * 2**20
         ),
         cost_estimate=pl.CostEstimate(flops=3 * 2 * 1008 * 2048 * 2048, bytes_accessed=2 * 2**24, transcendentals=0),
-    )(amplitudes.T, integrals.T, residual_in)[0]
+    )(amplitudes.T, integrals.T)[0]
+    return residual_in + ladder
 
 
 def solution(mesh):

time: 240 us -> 227 us (0.946)
  the two profiles are of different devices: /device:TPU:6 before, /device:TPU:32 now
where the time goes in v3:
time: 227 us; the launch traced here: 225 us
  Pallas kernels  223 us (98%)
    pallas_call x1, Pallas kernels, body(): pl.pallas_call(kernel, name='ladder', out_shape=(jax.ShapeDtypeStruct(res...  223 us

profile of v3, /device:TPU:32, one launch (start us, length us, event | category | flops | bytes accessed | tf_op | source)
XLA Modules:
  0.0 225.0 jit_solution(11412376744112724137)
XLA Ops:
  0.0 0.0 copy-start
  0.0 223.4 %ladder.1 = (f32[252,128]{1,0:T(8,128)}, f32[2,1024,256]{2,1,0:T(8,128)}, f32[2,2,1024,128]{3,2,1,0:T(8,128)}) custom-call(f32[8176,252]{1,0:T(8,128)} %bitcast.2, f32[8176,256]{1,0:T(8,128)} %bitcast.3), custom_call_target="tpu_custom_call" | custom-call | flops 25367150592 | bytes 33554432 | tf_op jit(solution)/shard_map/ladder/pallas_call | solution.py:498
  223.4 0.0 copy-done
  223.4 1.6 add.3
Async XLA Ops:
  0.0 223.4 %copy-start = (f32[252,128]{1,0:T(8,128)S(1)}, f32[252,128]{1,0:T(8,128)}, u32[]{:S(2)}) copy-start(f32[252,128]{1,0:T(8,128)} %param.5) | copy-start | bytes 387076

commit v4 on v3

--- a/solution.py
+++ b/solution.py
@@ -311,9 +311,9 @@
         send_near("v", half)
         sized(half * PART, PART, x, lambda local, whole, half=half: remote(
             itg.at[whole], vz.at[0, local], fsend.at[0, half], frecv.at[0, half], at(dzl=1)))
-    send_near("a", 0)
     for way in range(2):
         start_v(way)
+    send_near("a", 0)
     send_near("a", 1)
     for u in range(2):
         load_v(u, begin)
@@ -433,9 +433,7 @@
     last_tiles(1, 3)
     last_tiles(1, 1, half=0)
     take_far(1)
-    tiles(0, 7, lambda k: (3, k), half=1, free=SLOTS)
-    last_tiles(0, 1, half=1)
-    last_tiles(1, 1, half=1)
+    tiles(0, 8, lambda k: (3, k), half=1, free=SLOTS)
 
     @pl.when(late & (core == 1))
     def _():
@@ -471,7 +469,7 @@
 
         @pl.when(core != side)
         def _():
-            for i, half in [(0, None)] + parts:
+            for i, half in [(0, None)] + parts[:3]:
                 wait(plast.at[side, i, rows_of(half)], lsend.at[side, sem_row(i, half)])
 
     for half in range(2):

time: 227 us -> 224 us (0.987)
    pallas_call x1, Pallas kernels: 223 us -> 221 us  [body(): pl.pallas_call(kernel, name='ladder', out_shape=(jax.ShapeDtypeStruct(res...]
where the time goes in v4:
time: 224 us; the launch traced here: 223 us
  Pallas kernels  221 us (99%)
    pallas_call x1, Pallas kernels, body(): pl.pallas_call(kernel, name='ladder', out_shape=(jax.ShapeDtypeStruct(res...  221 us

profile of v4, /device:TPU:32, one launch (start us, length us, event | category | flops | bytes accessed | tf_op | source)
XLA Modules:
  0.0 222.6 jit_solution(6030375381945282916)
XLA Ops:
  0.0 0.0 copy-start
  0.0 221.0 %ladder.1 = (f32[252,128]{1,0:T(8,128)}, f32[2,1024,256]{2,1,0:T(8,128)}, f32[2,2,1024,128]{3,2,1,0:T(8,128)}) custom-call(f32[8176,252]{1,0:T(8,128)} %bitcast.2, f32[8176,256]{1,0:T(8,128)} %bitcast.3), custom_call_target="tpu_custom_call" | custom-call | flops 25367150592 | bytes 33554432 | tf_op jit(solution)/shard_map/ladder/pallas_call | solution.py:496
  221.0 0.0 copy-done
  221.0 1.6 add.3
Async XLA Ops:
  0.0 221.0 %copy-start = (f32[252,128]{1,0:T(8,128)S(1)}, f32[252,128]{1,0:T(8,128)}, u32[]{:S(2)}) copy-start(f32[252,128]{1,0:T(8,128)} %param.5) | copy-start | bytes 387076

commit v5 on v4

--- a/solution.py
+++ b/solution.py
@@ -446,20 +446,26 @@
 
     keep = lax.rem(zl + zh, 2)
     parts = [(i, None) for i in (1, 2)] + [(3, half) for half in range(2)]
-    for zj in range(2):
-        for i, half in parts:
+    def arrived(zj, some):
+        for i, half in some:
             wait(xrecv.at[(None, 1, 0, 2)[i], zj, rows_of(half)], orecv.at[sem_row(i, half) - 1, zj])
 
-    def summed(zj):
-        return (total[zj, 0] + xrecv[0, zj]) + (xrecv[1, zj] + xrecv[2, zj])
-
-    zsend[...] = summed(1 - keep)
-    remote(zsend, zrecv, zsem.at[0], zsem.at[1], at(dzh=1))
-    result = summed(keep)[: out.shape[0]]
-    wait(zrecv, zsem.at[1])
+    def summed(zj, rows):
+        return (total[zj, 0, rows] + xrecv[0, zj, rows]) + (xrecv[1, zj, rows] + xrecv[2, zj, rows])
+
+    for half in range(2):
+        rows = rows_of(half)
+        arrived(1 - keep, parts[:3] if half == 0 else parts[3:])
+        zsend[rows] = summed(1 - keep, rows)
+        remote(zsend.at[rows], zrecv.at[rows], zsem.at[0, half], zsem.at[1, half], at(dzh=1))
+    arrived(keep, parts)
+    result = summed(keep, rows_of(None))[: out.shape[0]]
+    for half in range(2):
+        wait(zrecv.at[rows_of(half)], zsem.at[1, half])
     out[...] = result + zrecv[: out.shape[0]]
 
-    wait(zsend, zsem.at[0])
+    for half in range(2):
+        wait(zsend.at[rows_of(half)], zsem.at[0, half])
     wait(yrecv, ysend)
     settle(HALF)
     for zj in range(2):
@@ -544,7 +550,7 @@
             dma((3, 2, 5)),
             dma((4, 2)),
             dma((4, 2)),
-            dma((2,)),
+            dma((2, 2)),
         ],
         compiler_params=pltpu.CompilerParams(
             collective_id=0, has_side_effects=True, vmem_limit_bytes=61 * 2**20

time: 224 us -> 222 us (level)
  no operation moved by 1% of the time
where the time goes in v5:
time: 222 us
  Pallas kernels  220 us (99%)
    pallas_call x1, Pallas kernels, body(): pl.pallas_call(kernel, name='ladder', out_shape=(jax.ShapeDtypeStruct(res...  220 us

profile of v5, /device:TPU:32, one launch (start us, length us, event | category | flops | bytes accessed | tf_op | source)
XLA Modules:
  0.0 221.7 jit_solution(15233519631483372607)
XLA Ops:
  0.0 0.0 copy-start
  0.0 220.1 %ladder.1 = (f32[252,128]{1,0:T(8,128)}, f32[2,1024,256]{2,1,0:T(8,128)}, f32[2,2,1024,128]{3,2,1,0:T(8,128)}) custom-call(f32[8176,252]{1,0:T(8,128)} %bitcast.2, f32[8176,256]{1,0:T(8,128)} %bitcast.3), custom_call_target="tpu_custom_call" | custom-call | flops 25367150592 | bytes 33554432 | tf_op jit(solution)/shard_map/ladder/pallas_call | solution.py:502
  220.1 0.0 copy-done
  220.2 1.6 add.3
Async XLA Ops:
  0.0 220.1 %copy-start = (f32[252,128]{1,0:T(8,128)S(1)}, f32[252,128]{1,0:T(8,128)}, u32[]{:S(2)}) copy-start(f32[252,128]{1,0:T(8,128)} %param.5) | copy-start | bytes 387076

commit v6 on v5

--- a/solution.py
+++ b/solution.py
@@ -400,6 +400,9 @@
 
     for way in range(2):
         pass_a(0, way)
+    for way in range(2):
+        pass_a(1, way)
+
     for i in (1, 2, 0):
         collect(0, i)
 
@@ -408,8 +411,6 @@
         for i in (1, 2, 0):
             collect(1, i)
 
-    for way in range(2):
-        pass_a(1, way)
     take_last(0)
     last_tiles(0, 3)
     take_far(0)

time: 222 us -> 222 us (level)
  no operation moved by 1% of the time
where the time goes in v6:
time: 222 us
  Pallas kernels  220 us (99%)
    pallas_call x1, Pallas kernels, body(): pl.pallas_call(kernel, name='ladder', out_shape=(jax.ShapeDtypeStruct(res...  220 us

profile of v6, /device:TPU:32, one launch (start us, length us, event | category | flops | bytes accessed | tf_op | source)
XLA Modules:
  0.0 221.7 jit_solution(8841622178877549656)
XLA Ops:
  0.0 0.0 copy-start
  0.0 220.1 %ladder.1 = (f32[252,128]{1,0:T(8,128)}, f32[2,1024,256]{2,1,0:T(8,128)}, f32[2,2,1024,128]{3,2,1,0:T(8,128)}) custom-call(f32[8176,252]{1,0:T(8,128)} %bitcast.2, f32[8176,256]{1,0:T(8,128)} %bitcast.3), custom_call_target="tpu_custom_call" | custom-call | flops 25367150592 | bytes 33554432 | tf_op jit(solution)/shard_map/ladder/pallas_call | solution.py:503
  220.1 0.0 copy-done
  220.2 1.6 add.3
Async XLA Ops:
  0.0 220.1 %copy-start = (f32[252,128]{1,0:T(8,128)S(1)}, f32[252,128]{1,0:T(8,128)}, u32[]{:S(2)}) copy-start(f32[252,128]{1,0:T(8,128)} %param.5) | copy-start | bytes 387076
